TPU v7x, 512 devices: a whole 4x4x16 slice. The times are simulated.
512 devices in a mesh: layer: 32 (over x, y, core), dp: 16 (over z).
Axes of the slice: x: 4, y: 4, z: 16, core: 2. Of those that a mesh axis runs over, the one named last changes fastest.
Arguments:
- weights: bfloat16 [128, 512, 512], P('layer', 'dp'), may hold values from -0.25 to 0.25
- biases: float32 [128, 512], P('layer'), may hold values from -3 to 3
- guesses: float32 [32, 8192, 512], P('layer', 'dp'), may hold values from -6 to 6
Outputs:
- states: bfloat16 [128, 8192, 512], P('layer', 'dp')
All inputs are finite; a program needn't handle non-finite values.
Results may differ from a plain program's by a relative error of at most 0.0041.
Values may be sent and summed in bfloat16 or wider, within the bound.
A program may use at most 64 MiB of HBM per device.

v0:
```python
import jax
import jax.numpy as jnp
from jax import lax
from jax.sharding import PartitionSpec as P

GROUP = 4


def copy_for_each(x, axis):
    count = lax.axis_size(axis)
    return lax.all_to_all(jnp.broadcast_to(x[None], (count, *x.shape)), axis, 0, 0, tiled=True)


def in_order(parts, dim):
    lengths = list(parts.shape[1:])
    lengths[dim] *= parts.shape[0]
    return jnp.moveaxis(parts, 0, dim).reshape(lengths)


def gathered_copies(x, axis, dim):
    parts = copy_for_each(x, axis)
    return in_order(parts, dim)


def from_behind(value, axis, steps):
    count = lax.axis_size(axis)
    initial, last = (max(0, -steps), min(count, count - steps))
    return lax.ppermute(value, axis, [(source, source + steps) for source in range(initial, last)])


def advance(states_in, weight_mat, bias_row, step_width):
    preact = jnp.dot(states_in.astype(jnp.bfloat16), weight_mat, preferred_element_type=jnp.float32)
    return states_in + step_width * jnp.tanh(preact + bias_row)


def take_phase(rows_all, phase):
    grouped = rows_all.reshape(rows_all.shape[0] // GROUP, GROUP, rows_all.shape[1])
    return lax.dynamic_index_in_dim(grouped, phase, 1, keepdims=False)


def put_phase(rows_all, phase, values):
    grouped = rows_all.reshape(rows_all.shape[0] // GROUP, GROUP, rows_all.shape[1])
    grouped = lax.dynamic_update_index_in_dim(grouped, values, phase, 1)
    return grouped.reshape(rows_all.shape)


def per_device(weights, biases, guesses):
    layer_count = lax.axis_size("layer")
    layer_depth = weights.shape[0]
    layer_rank = lax.axis_index("layer")
    own_phase = layer_rank % GROUP
    leader_rank = layer_rank // GROUP
    leaders = layer_count // GROUP
    fine_width = 4.0 / (layer_depth * layer_count)
    block_width = layer_depth * fine_width
    group_width = GROUP * block_width
    full_weights = gathered_copies(weights, "dp", 1)
    head_weight = full_weights[0]
    head_bias = biases[0]
    initial = guesses[0]

    def head_step(states_in, step_width):
        return advance(states_in, head_weight, head_bias, step_width)

    current = initial
    for layer_no in range(layer_depth):
        current = advance(current, full_weights[layer_no], biases[layer_no], fine_width)
    tau_one = from_behind(current - head_step(initial, block_width), "layer", 1)
    own_guess = take_phase(initial, own_phase)
    level = initial
    for member in range(1, GROUP + 1):
        outgoing = head_step(take_phase(level, (layer_rank + 1 - member) % GROUP), block_width)
        incoming = from_behind(outgoing, "layer", 1)
        landing = (layer_rank - member) % GROUP
        moved = incoming + take_phase(tau_one, landing)
        if member < GROUP:
            level = jnp.where(layer_rank >= 1, put_phase(level, landing, moved), level)
    behind = from_behind(head_step(own_guess, group_width), "layer", GROUP)
    tau_two = moved - behind
    coarse_state = jnp.where(layer_rank == 0, own_guess, moved)

    def leader_hop(turn_no, leader_state):
        arrived = from_behind(head_step(leader_state, group_width), "layer", GROUP)
        return jnp.where(leader_rank == turn_no, arrived + tau_two, leader_state)

    coarse_state = lax.fori_loop(1, leaders, leader_hop, coarse_state)
    corrected = put_phase(initial, own_phase, coarse_state)
    for member in range(1, GROUP):
        outgoing = head_step(take_phase(corrected, (layer_rank + 1 - member) % GROUP), block_width)
        incoming = from_behind(outgoing, "layer", 1)
        landing = (layer_rank - member) % GROUP
        renewed = incoming + take_phase(tau_one, landing)
        corrected = jnp.where(layer_rank >= 1, put_phase(corrected, landing, renewed), corrected)
    outputs = []
    current = corrected
    for layer_no in range(layer_depth):
        current = advance(current, full_weights[layer_no], biases[layer_no], fine_width)
        outputs.append(current.astype(jnp.bfloat16))
    return jnp.stack(outputs)


def solution(mesh):
    in_specs = (P("layer", "dp", None), P("layer", None), P("layer", "dp", None))
    out_specs = P("layer", "dp", None)
    return jax.shard_map(
        per_device, mesh=mesh, in_specs=in_specs, out_specs=out_specs, check_vma=False
    )
```

profile of v0, /device:TPU:6, one launch (start us, length us, event | category | flops | bytes accessed | tf_op | source)
XLA Modules:
  0.0 308.3 jit_solution(16958319518189660745)
XLA Ops:
  0.0 2.5 broadcast_in_dim.28
  2.5 15.3 %all-to-all-start = ((bf16[16,4,32,512]{3,2,1,0:T(8,128)(2,1)}), bf16[16,4,32,512]{3,2,1,0:T(8,128)(2,1)S(1)}, u32[]{:S(2)}, u32[]{:S(2)}) async-start(bf16[16,4,32,512]{3,2,1,0:T(8,128)(2,1)} %broadcast_in_dim.28), calls=%async_computation | async-start | bytes 4194304 | tf_op jit(solution)/shard_map/all_to_all | solution.py:11
  17.8 95.6 %all-to-all-done = bf16[16,4,32,512]{3,2,1,0:T(8,128)(2,1)S(1)} async-done(((bf16[16,4,32,512]{3,2,1,0:T(8,128)(2,1)}), bf16[16,4,32,512]{3,2,1,0:T(8,128)(2,1)S(1)}, u32[]{:S(2)}, u32[]{:S(2)}) %all-to-all-start) | async-done | bytes 2097184 | tf_op jit(solution)/shard_map/all_to_all | solution.py:11
  124.0 3.6 %collective-permute-start.1 = (f32[128,512]{1,0:T(8,128)}, f32[128,512]{1,0:T(8,128)}, u32[]{:S(2)}, u32[]{:S(2)}) collective-permute-start(f32[128,512]{1,0:T(8,128)} %get-tuple-element.140), channel_id=1, source_target_pairs={{0,16},{16,32},{32,48},{48,64},{64,80},{80,96},{96,112},{112,128},... | collective-permute-start | bytes 786440 | tf_op jit(solution)/shard_map/ppermute | solution.py:28
  129.4 8.8 %collective-permute-done.2 = f32[512,512]{1,0:T(8,128)} collective-permute-done((f32[512,512]{1,0:T(8,128)}, f32[512,512]{1,0:T(8,128)}, u32[]{:S(2)}, u32[]{:S(2)}) %collective-permute-start.2) | collective-permute-done | bytes 1048608 | tf_op jit(solution)/shard_map/ppermute | solution.py:28
  138.2 2.5 reshape.54
  140.7 4.4 %constant_dynamic-slice_fusion = (f32[128,1,512]{2,1,0:T(1,128)}, f32[128,1,512]{2,1,0:T(1,128)S(1)}, f32[128,1,512]{2,1,0:T(1,128)S(1)}, f32[128,1,512]{2,1,0:T(1,128)S(1)}) fusion(f32[128,4,512]{2,1,0:T(4,128)} %reshape.54, s32[]{:T(128)S(6)} %select_n.183, s32[]{:T(128)S(6)} %select_n.178, s32[]{:T(128)S(6)} %select_n.173, s32[]{:T(128)S(6)} %select_n.168), kind=kLoop, calls=%fused_computation.118 | loop fusion | bytes 2097168 | tf_op jit(solution)/shard_map/jit(dynamic_index_in_dim)/dynamic_slice | solution.py:38
  146.5 1.9 collective-permute-start.3
  148.5 7.9 %collective-permute-done.3 = f32[128,512]{1,0:T(8,128)S(1)} collective-permute-done((f32[128,512]{1,0:T(8,128)S(1)}, f32[128,512]{1,0:T(8,128)S(1)}, u32[]{:S(2)}, u32[]{:S(2)}) %collective-permute-start.3) | collective-permute-done | bytes 262176 | tf_op jit(solution)/shard_map/ppermute | solution.py:28
  158.6 1.9 collective-permute-start.6
  160.6 9.9 %collective-permute-done.4 = f32[128,512]{1,0:T(8,128)S(1)} collective-permute-done((f32[128,512]{1,0:T(8,128)S(1)}, f32[128,512]{1,0:T(8,128)S(1)}, u32[]{:S(2)}, u32[]{:S(2)}) %collective-permute-start.4) | collective-permute-done | bytes 262176 | tf_op jit(solution)/shard_map/ppermute | solution.py:28
  173.5 8.9 %collective-permute-done.5 = f32[128,512]{1,0:T(8,128)S(1)} collective-permute-done((f32[128,512]{1,0:T(8,128)}, f32[128,512]{1,0:T(8,128)S(1)}, u32[]{:S(2)}, u32[]{:S(2)}) %collective-permute-start.5) | collective-permute-done | bytes 262176 | tf_op jit(solution)/shard_map/ppermute | solution.py:28
  183.6 84.7 %while.13 = (s32[]{:T(128)}, f32[128,512]{1,0:T(8,128)S(1)}, s32[]{:T(128)}, bf16[512,512]{1,0:T(8,128)(2,1)S(1)}, f32[1,512]{1,0:T(1,128)S(1)}, /*index=5*/f32[128,512]{1,0:T(8,128)S(1)}, s32[]{:T(128)}) while((s32[]{:T(128)}, f32[128,512]{1,0:T(8,128)S(1)}, s32[]{:T(128)}, bf16[512,512]{1,0:T(8,128)(2,1)S(1)}, f32[1,512]{1,0:T(1,128)S(1)}, ...), condition=%wide.region_1.2_spmd, body=%wide.region_0.1_spmd.sunk | while | flops 67502080 | bytes 3147903 | solution.py:86
  183.9 1.9 collective-permute-start
  185.8 9.8 %collective-permute-done = f32[128,512]{1,0:T(8,128)S(1)} collective-permute-done((f32[128,512]{1,0:T(8,128)S(1)}, f32[128,512]{1,0:T(8,128)S(1)}, u32[]{:S(2)}, u32[]{:S(2)}) %collective-permute-start) | collective-permute-done | bytes 262176 | tf_op jit(solution)/shard_map/while/body/eval_jaxpr/ppermute | solution.py:28
  197.9 11.0 %collective-permute-done = f32[128,512]{1,0:T(8,128)S(1)} collective-permute-done((f32[128,512]{1,0:T(8,128)S(1)}, f32[128,512]{1,0:T(8,128)S(1)}, u32[]{:S(2)}, u32[]{:S(2)}) %collective-permute-start) | collective-permute-done | bytes 262176 | tf_op jit(solution)/shard_map/while/body/eval_jaxpr/ppermute | solution.py:28
  211.2 10.9 %collective-permute-done = f32[128,512]{1,0:T(8,128)S(1)} collective-permute-done((f32[128,512]{1,0:T(8,128)S(1)}, f32[128,512]{1,0:T(8,128)S(1)}, u32[]{:S(2)}, u32[]{:S(2)}) %collective-permute-start) | collective-permute-done | bytes 262176 | tf_op jit(solution)/shard_map/while/body/eval_jaxpr/ppermute | solution.py:28
  224.5 10.1 %collective-permute-done = f32[128,512]{1,0:T(8,128)S(1)} collective-permute-done((f32[128,512]{1,0:T(8,128)S(1)}, f32[128,512]{1,0:T(8,128)S(1)}, u32[]{:S(2)}, u32[]{:S(2)}) %collective-permute-start) | collective-permute-done | bytes 262176 | tf_op jit(solution)/shard_map/while/body/eval_jaxpr/ppermute | solution.py:28
  236.9 9.2 %collective-permute-done = f32[128,512]{1,0:T(8,128)S(1)} collective-permute-done((f32[128,512]{1,0:T(8,128)S(1)}, f32[128,512]{1,0:T(8,128)S(1)}, u32[]{:S(2)}, u32[]{:S(2)}) %collective-permute-start) | collective-permute-done | bytes 262176 | tf_op jit(solution)/shard_map/while/body/eval_jaxpr/ppermute | solution.py:28
  248.4 8.7 %collective-permute-done = f32[128,512]{1,0:T(8,128)S(1)} collective-permute-done((f32[128,512]{1,0:T(8,128)S(1)}, f32[128,512]{1,0:T(8,128)S(1)}, u32[]{:S(2)}, u32[]{:S(2)}) %collective-permute-start) | collective-permute-done | bytes 262176 | tf_op jit(solution)/shard_map/while/body/eval_jaxpr/ppermute | solution.py:28
  259.5 8.7 %collective-permute-done = f32[128,512]{1,0:T(8,128)S(1)} collective-permute-done((f32[128,512]{1,0:T(8,128)S(1)}, f32[128,512]{1,0:T(8,128)S(1)}, u32[]{:S(2)}, u32[]{:S(2)}) %collective-permute-start) | collective-permute-done | bytes 262176 | tf_op jit(solution)/shard_map/while/body/eval_jaxpr/ppermute | solution.py:28
  270.5 7.9 %collective-permute-done.7 = f32[128,512]{1,0:T(8,128)S(1)} collective-permute-done((f32[128,512]{1,0:T(8,128)S(1)}, f32[128,512]{1,0:T(8,128)S(1)}, u32[]{:S(2)}, u32[]{:S(2)}) %collective-permute-start.7) | collective-permute-done | bytes 262176 | tf_op jit(solution)/shard_map/ppermute | solution.py:28
  281.6 7.9 %collective-permute-done.8 = f32[128,512]{1,0:T(8,128)S(1)} collective-permute-done((f32[128,512]{1,0:T(8,128)S(1)}, f32[128,512]{1,0:T(8,128)S(1)}, u32[]{:S(2)}, u32[]{:S(2)}) %collective-permute-start.8) | collective-permute-done | bytes 262176 | tf_op jit(solution)/shard_map/ppermute | solution.py:28
  291.8 7.9 %collective-permute-done.9 = f32[128,512]{1,0:T(8,128)S(1)} collective-permute-done((f32[128,512]{1,0:T(8,128)S(1)}, f32[128,512]{1,0:T(8,128)S(1)}, u32[]{:S(2)}, u32[]{:S(2)}) %collective-permute-start.9) | collective-permute-done | bytes 262176 | tf_op jit(solution)/shard_map/ppermute | solution.py:28
  (89 shorter events, 50.2 us)
Async XLA Ops:
  2.5 15.3 %copy-start.11 = (f32[4,512]{1,0:T(4,128)S(1)}, f32[4,512]{1,0:T(4,128)}, u32[]{:S(2)}) copy-start(f32[4,512]{1,0:T(4,128)} %param.6) | copy-start | bytes 24580
  2.5 110.9 %all-to-all-start = ((bf16[16,4,32,512]{3,2,1,0:T(8,128)(2,1)}), bf16[16,4,32,512]{3,2,1,0:T(8,128)(2,1)S(1)}, u32[]{:S(2)}, u32[]{:S(2)}) async-start(bf16[16,4,32,512]{3,2,1,0:T(8,128)(2,1)} %broadcast_in_dim.28), calls=%async_computation | async-start | bytes 4194304 | tf_op jit(solution)/shard_map/all_to_all | solution.py:11
  114.7 1.9 copy-start
  116.5 1.5 copy-start.9
  119.6 18.5 %collective-permute-start.2 = (f32[512,512]{1,0:T(8,128)}, f32[512,512]{1,0:T(8,128)}, u32[]{:S(2)}, u32[]{:S(2)}) collective-permute-start(f32[512,512]{1,0:T(8,128)} %fusion.19), channel_id=1, source_target_pairs={{0,16},{16,32},{32,48},{48,64},{64,80},{80,96},{96,112},{112,128},... | collective-permute-start | bytes 3145736 | tf_op jit(solution)/shard_map/ppermute | solution.py:28
  121.9 5.8 %copy-start.2 = (f32[128,4,512]{2,1,0:T(4,128)}, f32[128,4,512]{2,1,0:T(4,128)S(1)}, u32[]{:S(2)}) copy-start(f32[128,4,512]{2,1,0:T(4,128)S(1)} %reshape_squeeze.2) | copy-start | bytes 3145732
  124.0 21.0 %collective-permute-start.1 = (f32[128,512]{1,0:T(8,128)}, f32[128,512]{1,0:T(8,128)}, u32[]{:S(2)}, u32[]{:S(2)}) collective-permute-start(f32[128,512]{1,0:T(8,128)} %get-tuple-element.140), channel_id=1, source_target_pairs={{0,16},{16,32},{32,48},{48,64},{64,80},{80,96},{96,112},{112,128},... | collective-permute-start | bytes 786440 | tf_op jit(solution)/shard_map/ppermute | solution.py:28
  145.0 11.6 %copy-start.5 = (f32[128,1,512]{2,1,0:T(1,128)}, f32[128,1,512]{2,1,0:T(1,128)S(1)}, u32[]{:S(2)}) copy-start(f32[128,1,512]{2,1,0:T(1,128)S(1)} %get-tuple-element.135) | copy-start | bytes 786436
  145.1 11.6 %copy-start.7 = (f32[128,1,512]{2,1,0:T(1,128)}, f32[128,1,512]{2,1,0:T(1,128)S(1)}, u32[]{:S(2)}) copy-start(f32[128,1,512]{2,1,0:T(1,128)S(1)} %get-tuple-element.136) | copy-start | bytes 786436
  146.5 9.8 %collective-permute-start.3 = (f32[128,512]{1,0:T(8,128)S(1)}, f32[128,512]{1,0:T(8,128)S(1)}, u32[]{:S(2)}, u32[]{:S(2)}) collective-permute-start(f32[128,512]{1,0:T(8,128)S(1)} %fusion.47), channel_id=1, source_target_pairs={{0,16},{16,32},{32,48},{48,64},{64,80},{80,96},{96,112},{112,128},... | collective-permute-start | bytes 786440 | tf_op jit(solution)/shard_map/ppermute | solution.py:28
  156.7 13.8 %collective-permute-start.4 = (f32[128,512]{1,0:T(8,128)S(1)}, f32[128,512]{1,0:T(8,128)S(1)}, u32[]{:S(2)}, u32[]{:S(2)}) collective-permute-start(f32[128,512]{1,0:T(8,128)S(1)} %fusion.46), channel_id=1, source_target_pairs={{0,16},{16,32},{32,48},{48,64},{64,80},{80,96},{96,112},{112,128},... | collective-permute-start | bytes 786440 | tf_op jit(solution)/shard_map/ppermute | solution.py:28
  158.6 14.8 %collective-permute-start.6 = (f32[128,512]{1,0:T(8,128)}, f32[128,512]{1,0:T(8,128)}, u32[]{:S(2)}, u32[]{:S(2)}) collective-permute-start(f32[128,512]{1,0:T(8,128)} %get-tuple-element.139), channel_id=1, source_target_pairs={{0,64},{16,80},{32,96},{48,112},{64,128},{80,144},{96,160},{112,17... | collective-permute-start | bytes 786440 | tf_op jit(solution)/shard_map/ppermute | solution.py:28
  171.5 10.9 %collective-permute-start.5 = (f32[128,512]{1,0:T(8,128)}, f32[128,512]{1,0:T(8,128)S(1)}, u32[]{:S(2)}, u32[]{:S(2)}) collective-permute-start(f32[128,512]{1,0:T(8,128)} %fusion.45), channel_id=1, source_target_pairs={{0,16},{16,32},{32,48},{48,64},{64,80},{80,96},{96,112},{112,128},... | collective-permute-start | bytes 786440 | tf_op jit(solution)/shard_map/ppermute | solution.py:28
  183.9 11.7 %collective-permute-start = (f32[128,512]{1,0:T(8,128)S(1)}, f32[128,512]{1,0:T(8,128)S(1)}, u32[]{:S(2)}, u32[]{:S(2)}) collective-permute-start(f32[128,512]{1,0:T(8,128)S(1)} %fusion.111), channel_id=1, source_target_pairs={{0,64},{16,80},{32,96},{48,112},{64,128},{80,144},{96,160},{112,17... | collective-permute-start | bytes 786440 | tf_op jit(solution)/shard_map/while/body/eval_jaxpr/ppermute | solution.py:28
  196.0 12.9 %collective-permute-start = (f32[128,512]{1,0:T(8,128)S(1)}, f32[128,512]{1,0:T(8,128)S(1)}, u32[]{:S(2)}, u32[]{:S(2)}) collective-permute-start(f32[128,512]{1,0:T(8,128)S(1)} %fusion.111), channel_id=1, source_target_pairs={{0,64},{16,80},{32,96},{48,112},{64,128},{80,144},{96,160},{112,17... | collective-permute-start | bytes 786440 | tf_op jit(solution)/shard_map/while/body/eval_jaxpr/ppermute | solution.py:28
  209.3 12.9 %collective-permute-start = (f32[128,512]{1,0:T(8,128)S(1)}, f32[128,512]{1,0:T(8,128)S(1)}, u32[]{:S(2)}, u32[]{:S(2)}) collective-permute-start(f32[128,512]{1,0:T(8,128)S(1)} %fusion.111), channel_id=1, source_target_pairs={{0,64},{16,80},{32,96},{48,112},{64,128},{80,144},{96,160},{112,17... | collective-permute-start | bytes 786440 | tf_op jit(solution)/shard_map/while/body/eval_jaxpr/ppermute | solution.py:28
  222.5 12.1 %collective-permute-start = (f32[128,512]{1,0:T(8,128)S(1)}, f32[128,512]{1,0:T(8,128)S(1)}, u32[]{:S(2)}, u32[]{:S(2)}) collective-permute-start(f32[128,512]{1,0:T(8,128)S(1)} %fusion.111), channel_id=1, source_target_pairs={{0,64},{16,80},{32,96},{48,112},{64,128},{80,144},{96,160},{112,17... | collective-permute-start | bytes 786440 | tf_op jit(solution)/shard_map/while/body/eval_jaxpr/ppermute | solution.py:28
  235.0 11.2 %collective-permute-start = (f32[128,512]{1,0:T(8,128)S(1)}, f32[128,512]{1,0:T(8,128)S(1)}, u32[]{:S(2)}, u32[]{:S(2)}) collective-permute-start(f32[128,512]{1,0:T(8,128)S(1)} %fusion.111), channel_id=1, source_target_pairs={{0,64},{16,80},{32,96},{48,112},{64,128},{80,144},{96,160},{112,17... | collective-permute-start | bytes 786440 | tf_op jit(solution)/shard_map/while/body/eval_jaxpr/ppermute | solution.py:28
  246.5 10.7 %collective-permute-start = (f32[128,512]{1,0:T(8,128)S(1)}, f32[128,512]{1,0:T(8,128)S(1)}, u32[]{:S(2)}, u32[]{:S(2)}) collective-permute-start(f32[128,512]{1,0:T(8,128)S(1)} %fusion.111), channel_id=1, source_target_pairs={{0,64},{16,80},{32,96},{48,112},{64,128},{80,144},{96,160},{112,17... | collective-permute-start | bytes 786440 | tf_op jit(solution)/shard_map/while/body/eval_jaxpr/ppermute | solution.py:28
  257.5 10.7 %collective-permute-start = (f32[128,512]{1,0:T(8,128)S(1)}, f32[128,512]{1,0:T(8,128)S(1)}, u32[]{:S(2)}, u32[]{:S(2)}) collective-permute-start(f32[128,512]{1,0:T(8,128)S(1)} %fusion.111), channel_id=1, source_target_pairs={{0,64},{16,80},{32,96},{48,112},{64,128},{80,144},{96,160},{112,17... | collective-permute-start | bytes 786440 | tf_op jit(solution)/shard_map/while/body/eval_jaxpr/ppermute | solution.py:28
  268.3 21.2 %copy-start.6 = (f32[128,1,512]{2,1,0:T(1,128)S(1)}, f32[128,1,512]{2,1,0:T(1,128)}, u32[]{:S(2)}) copy-start(f32[128,1,512]{2,1,0:T(1,128)} %copy-done.5) | copy-start | bytes 786436
  268.6 9.8 %collective-permute-start.7 = (f32[128,512]{1,0:T(8,128)S(1)}, f32[128,512]{1,0:T(8,128)S(1)}, u32[]{:S(2)}, u32[]{:S(2)}) collective-permute-start(f32[128,512]{1,0:T(8,128)S(1)} %fusion.44), channel_id=1, source_target_pairs={{0,16},{16,32},{32,48},{48,64},{64,80},{80,96},{96,112},{112,128},... | collective-permute-start | bytes 786440 | tf_op jit(solution)/shard_map/ppermute | solution.py:28
  279.7 9.8 %collective-permute-start.8 = (f32[128,512]{1,0:T(8,128)S(1)}, f32[128,512]{1,0:T(8,128)S(1)}, u32[]{:S(2)}, u32[]{:S(2)}) collective-permute-start(f32[128,512]{1,0:T(8,128)S(1)} %fusion.43), channel_id=1, source_target_pairs={{0,16},{16,32},{32,48},{48,64},{64,80},{80,96},{96,112},{112,128},... | collective-permute-start | bytes 786440 | tf_op jit(solution)/shard_map/ppermute | solution.py:28
  289.8 9.8 %collective-permute-start.9 = (f32[128,512]{1,0:T(8,128)S(1)}, f32[128,512]{1,0:T(8,128)S(1)}, u32[]{:S(2)}, u32[]{:S(2)}) collective-permute-start(f32[128,512]{1,0:T(8,128)S(1)} %fusion.42), channel_id=1, source_target_pairs={{0,16},{16,32},{32,48},{48,64},{64,80},{80,96},{96,112},{112,128},... | collective-permute-start | bytes 786440 | tf_op jit(solution)/shard_map/ppermute | solution.py:28
  (5 other events, 5.2 us)
where the time goes:
time: 309 us; the launch traced here: 308 us
  waiting for transfers between devices  223 us (72%)
  starting transfers between devices  47.7 us (15%)
  local copies, waits for them, and re-layouts  19.2 us (6%)
  matrix products  9.75 us (3%)
  other arithmetic  7.5 us (2%)
    ppermute x16, waiting for transfers between devices, from_behind(): lax.ppermute(value, axis, [(source, source + steps) for source in range(i...  128 us
    all_to_all x1, waiting for transfers between devices, copy_for_each(): lax.all_to_all(jnp.broadcast_to(x[None], (count, *x.shape)), axis, 0, 0,...  95.6 us
    ppermute x16, starting transfers between devices, from_behind(): lax.ppermute(value, axis, [(source, source + steps) for source in range(i...  32.4 us
    all_to_all x1, starting transfers between devices, copy_for_each(): lax.all_to_all(jnp.broadcast_to(x[None], (count, *x.shape)), axis, 0, 0,...  15.3 us
    dot_general x22, matrix products, advance(): jnp.dot(states_in.astype(jnp.bfloat16), weight_mat, preferred_element_typ...  9.75 us
  transfers between devices with their start and end apart: 17, of which 15 were waited for; matrix products, arithmetic and copies ran while one was open for 4% of the time, Pallas kernels for 0%

commit v1 on v0

v1 whole, which is shorter than its diff:
```python
import jax
import jax.numpy as jnp
from jax import lax
from jax.experimental import pallas as pl
from jax.experimental.pallas import tpu as pltpu
from jax.sharding import PartitionSpec as P

MESH = pl.DeviceIdType.MESH
GROUP = 4
NL = 32
NZ = 16
D = 512
ROWS = 512
PR = ROWS // GROUP
HR = PR // 2
KR = D // NZ
LD = 4
LANES = 128
FINE = 4.0 / 128
BLOCK = 4 * FINE
WIDE = 16 * FINE


def kernel(
    w_ref, b_ref, g_ref, o_ref,
    wf, natural, guess, tau, level_in, level_out, heads, hbias, arr, qg, taup,
    coarse_in, coarse_out, coarse, corr_other, first_out, first_in, hop_in, hop_out, fin,
    load_s, ring_s, ring_r, head_s, head_r, bias_s, bias_r, qg_s, qg_r, tau_s, tau_r, level_s, level_r,
    arr_s, arr_r, q_s, q_r, corr_s, corr_r, first_s, first_r, hop_s, hop_r,
):
    r = lax.axis_index("layer")
    z = lax.axis_index("dp")
    nxt = lax.rem(r + 1, NL)
    prv = lax.rem(r + NL - 1, NL)
    h = lax.rem(r // 4, 2)

    def flip(d):
        return d + 4 - 8 * lax.rem(d // 4, 2)

    mate = flip(r)
    x_next = lax.rem(r + 8, NL)
    x_prev = lax.rem(r + NL - 8, NL)
    mate_next = lax.rem(mate + 1, NL)
    next_mate = flip(nxt)
    hn = lax.rem(nxt // 4, 2)
    z_up = lax.rem(z + 1, NZ)
    z_dn = lax.rem(z + NZ - 1, NZ)

    def phase(back):
        return lax.rem(r - back + 2 * GROUP, GROUP)

    def to(layer, src, dst, send, recv):
        return pltpu.make_async_remote_copy(
            src_ref=src, dst_ref=dst, send_sem=send, recv_sem=recv,
            device_id=(layer, z), device_id_type=MESH)

    loads = [
        pltpu.make_async_copy(g_ref.at[0, :, pl.ds(c * LANES, LANES)], natural.at[c], load_s.at[c])
        for c in range(D // LANES)
    ]
    for load in loads:
        load.start()
    barrier = pltpu.get_barrier_semaphore()
    for dev in (
        (r, z_up), (r, z_dn), (nxt, z), (prv, z), (x_next, z), (x_prev, z), (mate, z),
        (mate_next, z), (flip(prv), z), (next_mate, z), (lax.rem(mate + NL - 1, NL), z),
    ):
        pl.semaphore_signal(barrier, inc=1, device_id=dev, device_id_type=MESH)

    mine = pl.ds(pl.multiple_of(z * KR, KR), KR)
    for layer in range(LD):
        wf[layer, mine, :] = w_ref[layer]
    pl.semaphore_wait(barrier, 11)

    def shard(layer, origin):
        o = lax.rem(origin + 2 * NZ, NZ)
        return wf.at[layer, pl.ds(pl.multiple_of(o * KR, KR), KR)]

    def ring(way, step, layer):
        origin = z - (step - 1) if way == 0 else z + (step - 1)
        part = shard(layer, origin)
        return pltpu.make_async_remote_copy(
            src_ref=part, dst_ref=part, send_sem=ring_s.at[way, step - 1, layer],
            recv_sem=ring_r.at[way, step - 1, layer],
            device_id=(r, z_up if way == 0 else z_dn), device_id_type=MESH)

    def ring_arrived(way, step, layer):
        origin = z - step if way == 0 else z + step
        part = shard(layer, origin)
        pltpu.make_async_remote_copy(
            src_ref=part, dst_ref=part, send_sem=ring_s.at[way, step - 1, layer],
            recv_sem=ring_r.at[way, step - 1, layer],
            device_id=(r, z_up if way == 0 else z_dn), device_id_type=MESH).wait_recv()

    def head_copy(origin, slot):
        o = lax.rem(origin + 2 * NZ, NZ)
        rows = pl.ds(pl.multiple_of(o * KR, KR), KR)
        return to(mate, wf.at[0, rows], heads.at[slot, rows], head_s.at[o], head_r.at[o])

    def last_step(way, layer):
        return (layer < 2) == (way == 0)

    for layer in range(LD):
        for way in range(2):
            ring(way, 1, layer).start()
    head_copy(z, h).start()
    bias_copy = to(mate, b_ref, hbias.at[h], bias_s.at[0], bias_r.at[0])
    bias_copy.start()
    hbias[h] = b_ref[...]
    for c in range(D // LANES):
        loads[c].wait()
        for p in range(GROUP):
            guess[p, :, pl.ds(c * LANES, LANES)] = natural[c, pl.ds(p, PR, stride=GROUP), :]

    def ring_body(step, carry):
        for layer in range(LD):
            for way in range(2):
                ring_arrived(way, step, layer)
                ring(way, step + 1, layer).start()
                if layer == 0:
                    head_copy(z - step if way == 0 else z + step, h).start()
        return carry

    lax.fori_loop(1, 7, ring_body, 0)
    for layer in range(LD):
        for way in range(2):
            ring_arrived(way, 7, layer)
            if last_step(way, layer):
                ring(way, 8, layer).start()
            if layer == 0:
                head_copy(z - 7 if way == 0 else z + 7, h).start()
    for layer in range(LD):
        for way in range(2):
            if last_step(way, layer):
                ring_arrived(way, 8, layer)
                if layer == 0:
                    head_copy(z - 8, h).start()

    def act(u, weight, bias):
        return jnp.tanh(jnp.dot(u.astype(jnp.bfloat16), weight, preferred_element_type=jnp.float32) + bias)

    def bias_row(layer):
        return b_ref[pl.ds(layer, 1), :]

    def half_rows(half):
        return pl.ds(pl.multiple_of(half * HR, HR), HR)

    def sweep(back):
        p = phase(back)
        start = guess[p]
        first = act(start, wf[0], bias_row(0))
        u = start + FINE * first
        for layer in range(1, LD):
            u = u + FINE * act(u, wf[layer], bias_row(layer))
        tau[p] = u - (start + BLOCK * first)
        return start, first, u

    def level_copy(m, c):
        rows = pl.ds(c * HR, HR)
        return to(nxt, level_out.at[m, rows], level_in.at[m, rows], level_s.at[m, c], level_r.at[m, c])

    start, first, end = sweep(0)
    level_out[0] = end
    for c in range(2):
        level_copy(0, c).start()
    level_out[4] = start + WIDE * first
    own_rows = half_rows(h)
    other_rows = half_rows(1 - h)
    qg[h] = level_out[4, own_rows, :]
    qg_copy = to(mate, level_out.at[4, other_rows], qg.at[h], qg_s.at[0], qg_r.at[0])
    qg_copy.start()
    taup[h] = tau[phase(0), own_rows, :]
    tau_copy = to(mate, tau.at[phase(0), other_rows], taup.at[h], tau_s.at[0], tau_r.at[0])
    tau_copy.start()
    own_head = pltpu.make_async_copy(wf.at[0], heads.at[h], bias_s.at[1])
    own_head.start()

    arr_near = to(nxt, level_out.at[3, half_rows(hn)], arr.at[hn], arr_s.at[0], arr_r.at[hn])
    arr_far = to(next_mate, level_out.at[3, half_rows(1 - hn)], arr.at[hn], arr_s.at[1], arr_r.at[hn])
    arr_start = to(mate, guess.at[0, pl.ds(HR, HR)], arr.at[0], arr_s.at[2], arr_r.at[0])

    @pl.when(r == 0)
    def _():
        arr_start.start()
        arr[0] = guess[0, pl.ds(0, HR), :]

    for m in range(1, 4):
        sweep(m)
        p = phase(m)
        for c in range(2):
            rows = pl.ds(c * HR, HR)
            level_copy(m - 1, c).wait_recv()
            u = jnp.where(r == 0, guess[p, rows, :], level_in[m - 1, rows, :])
            level_out[m, rows, :] = u + BLOCK * act(u, wf[0], bias_row(0)) + tau[p, rows, :]
            if m < 3:
                level_copy(m, c).start()
        if m == 3:
            @pl.when(r != NL - 1)
            def _():
                arr_near.start()
                arr_far.start()

    def wait_heads(o, carry):
        head_copy(o, h).wait_recv()
        return carry

    lax.fori_loop(0, NZ, wait_heads, 0)
    bias_copy.wait_recv()
    own_head.wait()
    qg_copy.wait_recv()
    tau_copy.wait_recv()

    def arrived(slot):
        to(nxt, level_out.at[3, pl.ds(0, HR)], arr.at[slot], arr_s.at[0], arr_r.at[slot]).wait_recv()

    @pl.when(jnp.logical_or(r != 0, h != 0))
    def _():
        arrived(0)

    arrived(1)
    x_pos = r // 8
    q_copy = to(x_next, coarse_out, coarse_in, q_s.at[0], q_r.at[0])

    @pl.when(x_pos == 0)
    def _():
        coarse[0] = arr[0]

    @pl.when(x_pos != 0)
    def _():
        q_copy.wait_recv()
        coarse[0] = arr[0] + coarse_in[...]

    ua = coarse[0]
    ta = act(ua, heads[0], hbias[0, pl.ds(0, 1), :])
    ub = arr[1] + ((ua + WIDE * ta) - qg[0])
    coarse[1] = ub
    tb = act(ub, heads[1], hbias[1, pl.ds(0, 1), :])

    @pl.when(x_pos != 3)
    def _():
        coarse_out[...] = (ub + WIDE * tb) - qg[1]
        q_copy.start()

    first_out[0] = ua + BLOCK * ta + taup[0]
    first_out[1] = ub + BLOCK * tb + taup[1]
    first_near = to(nxt, first_out.at[h], first_in.at[own_rows], first_s.at[0], first_r.at[h])
    first_far = to(mate_next, first_out.at[1 - h], first_in.at[own_rows], first_s.at[1], first_r.at[h])
    first_far.start()
    first_near.start()
    corr_copy = to(mate, coarse.at[1 - h], corr_other, corr_s.at[0], corr_r.at[0])
    corr_copy.start()

    def put(p, offset, count, values):
        for c in range(D // LANES):
            fin[c, pl.ds(p + GROUP * offset, count, stride=GROUP), :] = values[:, c * LANES:(c + 1) * LANES]

    put(phase(0), h * HR, HR, coarse[h])

    def hop(m, c):
        rows = pl.ds(c * HR, HR)
        return to(nxt, hop_out.at[m, rows], hop_in.at[m, rows], hop_s.at[m, c], hop_r.at[m, c])

    def first_arrived(half):
        to(nxt, first_out.at[0], first_in.at[half_rows(half)], first_s.at[0], first_r.at[half]).wait_recv()

    for m in range(1, 4):
        p = phase(m)
        for c in range(2):
            rows = pl.ds(c * HR, HR)
            if m == 1:
                first_arrived(c)
                got = first_in[rows, :]
            else:
                hop(m - 2, c).wait_recv()
                got = hop_in[m - 2, rows, :]
            u = jnp.where(r == 0, guess[p, rows, :], got)
            if m < 3:
                hop_out[m - 1, rows, :] = u + BLOCK * act(u, wf[0], bias_row(0)) + tau[p, rows, :]
                hop(m - 1, c).start()
            put(p, c * HR, HR, u)
    corr_copy.wait_recv()
    put(phase(0), (1 - h) * HR, HR, corr_other[...])

    for tile in range(4):
        rows = pl.ds(tile * 128, 128)
        u = jnp.concatenate([fin[c, rows, :] for c in range(D // LANES)], axis=1)
        for layer in range(LD):
            u = u + FINE * act(u, wf[layer], bias_row(layer))
            o_ref[layer, rows, :] = u.astype(jnp.bfloat16)

    def drain(step, carry):
        for layer in range(LD):
            for way in range(2):
                ring(way, step, layer).wait_send()
        return carry

    lax.fori_loop(1, 8, drain, 0)
    for layer in range(LD):
        for way in range(2):
            if last_step(way, layer):
                ring(way, 8, layer).wait_send()

    def drain_heads(o, carry):
        head_copy(o, h).wait_send()
        return carry

    lax.fori_loop(0, NZ, drain_heads, 0)
    bias_copy.wait_send()
    qg_copy.wait_send()
    tau_copy.wait_send()
    for m in range(3):
        for c in range(2):
            level_copy(m, c).wait_send()

    @pl.when(r == 0)
    def _():
        arr_start.wait_send()

    @pl.when(r != NL - 1)
    def _():
        arr_far.wait_send()
        arr_near.wait_send()

    @pl.when(x_pos != 3)
    def _():
        q_copy.wait_send()

    first_near.wait_send()
    first_far.wait_send()
    corr_copy.wait_send()
    for m in range(2):
        for c in range(2):
            hop(m, c).wait_send()


def per_device(weights, biases, guesses):
    f32, bf16 = jnp.float32, jnp.bfloat16
    dma = pltpu.SemaphoreType.DMA
    vmem = pl.BlockSpec(memory_space=pltpu.VMEM)
    scratch = [
        pltpu.VMEM((LD, D, D), bf16),
        pltpu.VMEM((D // LANES, ROWS, LANES), f32),
        pltpu.VMEM((GROUP, PR, D), f32),
        pltpu.VMEM((GROUP, PR, D), f32),
        pltpu.VMEM((3, PR, D), f32),
        pltpu.VMEM((5, PR, D), f32),
        pltpu.VMEM((2, D, D), bf16),
        pltpu.VMEM((2, LD, D), f32),
        pltpu.VMEM((2, HR, D), f32),
        pltpu.VMEM((2, HR, D), f32),
        pltpu.VMEM((2, HR, D), f32),
        pltpu.VMEM((HR, D), f32),
        pltpu.VMEM((HR, D), f32),
        pltpu.VMEM((2, HR, D), f32),
        pltpu.VMEM((HR, D), f32),
        pltpu.VMEM((2, HR, D), f32),
        pltpu.VMEM((PR, D), f32),
        pltpu.VMEM((2, PR, D), f32),
        pltpu.VMEM((2, PR, D), f32),
        pltpu.VMEM((D // LANES, ROWS, LANES), f32),
        dma((D // LANES,)),
        dma((2, 8, LD)), dma((2, 8, LD)),
        dma((NZ,)), dma((NZ,)),
        dma((2,)), dma((1,)),
        dma((1,)), dma((1,)),
        dma((1,)), dma((1,)),
        dma((3, 2)), dma((3, 2)),
        dma((3,)), dma((2,)),
        dma((1,)), dma((1,)),
        dma((1,)), dma((1,)),
        dma((2,)), dma((2,)),
        dma((2, 2)), dma((2, 2)),
    ]
    return pl.pallas_call(
        kernel,
        out_shape=jax.ShapeDtypeStruct((LD, ROWS, D), bf16),
        in_specs=[vmem, vmem, pl.BlockSpec(memory_space=pl.ANY)],
        out_specs=vmem,
        scratch_shapes=scratch,
        compiler_params=pltpu.CompilerParams(
            collective_id=1, has_side_effects=True, vmem_limit_bytes=48 * 2**20),
        cost_estimate=pl.CostEstimate(flops=3 * 10**9, bytes_accessed=3 * 2**20, transcendentals=3 * 10**6),
    )(weights, biases, guesses)


def solution(mesh):
    in_specs = (P("layer", "dp", None), P("layer", None), P("layer", "dp", None))
    out_specs = P("layer", "dp", None)
    return jax.shard_map(
        per_device, mesh=mesh, in_specs=in_specs, out_specs=out_specs, check_vma=False
    )
```

time: 309 us -> 96.8 us (0.31)
  the two profiles are of different devices: /device:TPU:6 before, /device:TPU:1 now
where the time goes in v1:
time: 96.8 us; the launch traced here: 96.6 us
  Pallas kernels  92.4 us (95%)
  local copies, waits for them, and re-layouts  4.15 us (4%)
    pallas_call x1, Pallas kernels, per_device(): pl.pallas_call(kernel, out_shape=jax.ShapeDtypeStruct((LD, ROWS, D), bf16...  92.4 us
    unnamed x7, local copies, waits for them, and re-layouts  4.15 us

profile of v1, /device:TPU:1, one launch (start us, length us, event | category | flops | bytes accessed | tf_op | source)
XLA Modules:
  0.0 96.6 jit_solution(516055876774362376)
XLA Ops:
  0.0 0.0 copy-start
  0.0 1.2 %copy-done = f32[1,512,512]{2,1,0:T(8,128)S(1)} copy-done((f32[1,512,512]{2,1,0:T(8,128)S(1)}, f32[1,512,512]{2,1,0:T(8,128)}, u32[]{:S(2)}) %copy-start) | copy-done | bytes 1048600
  1.2 0.0 copy-start.1
  1.2 0.9 copy-done.1
  2.1 0.0 copy-start.2
  2.1 0.7 copy-done.2
  2.8 92.4 %shard_map.37 = bf16[4,512,512]{2,1,0:T(8,128)(2,1)S(1)} custom-call(bf16[4,32,512]{2,1,0:T(8,128)(2,1)S(1)} %copy-done.1, f32[4,512]{1,0:T(4,128)S(1)} %copy-done.2, f32[1,512,512]{2,1,0:T(8,128)S(1)} %copy-done), custom_call_target="tpu_custom_call" | custom-call | flops 3000000000 | bytes 3145728 | tf_op jit(solution)/shard_map/pallas_call | solution.py:374
  95.2 1.3 %copy.5 = bf16[4,512,512]{2,1,0:T(8,128)(2,1)} copy(bf16[4,512,512]{2,1,0:T(8,128)(2,1)S(1)} %shard_map.37) | data formatting | bytes 4194304
Async XLA Ops:
  0.0 1.2 %copy-start = (f32[1,512,512]{2,1,0:T(8,128)S(1)}, f32[1,512,512]{2,1,0:T(8,128)}, u32[]{:S(2)}) copy-start(f32[1,512,512]{2,1,0:T(8,128)} %g_ref.1) | copy-start | bytes 3145732
  1.2 0.9 copy-start.1
  2.1 0.7 copy-start.2

commit v2 on v0

v2 whole, which is shorter than its diff:
```python
import jax
import jax.numpy as jnp
from jax import lax
from jax.experimental import pallas as pl
from jax.experimental.pallas import tpu as pltpu
from jax.sharding import PartitionSpec as P

MESH = pl.DeviceIdType.MESH
GROUP = 4
QUAD = 4
NL = 32
NZ = 16
D = 512
LANES = 128
ROWS = 512
PR = ROWS // GROUP
HR = PR // 2
QR = PR // QUAD
KR = D // NZ
LD = 4
FINE = 4.0 / 128
BLOCK = 4 * FINE
WIDE = 16 * FINE


def kernel(
    w_ref, b_ref, g_ref, o_ref,
    wf, bias, natural, guess, base_in, tau, inc_in, inc_out, heads, hbias, part, part_act, arr, base_far,
    coarse_in, coarse_out, coarse, corr_in, first_out, first_in, hop_in, hop_out, fin,
    load_s, ring_s, ring_r, head_s, head_r, bias_s, bias_r, part_s, part_r, base_s, base_r, far_s, far_r,
    level_s, level_r, arr_s, arr_r, q_s, q_r, corr_s, corr_r, first_s, first_r, hop_s, hop_r, own_s,
):
    r = lax.axis_index("layer")
    z = lax.axis_index("dp")
    nxt = lax.rem(r + 1, NL)
    prv = lax.rem(r + NL - 1, NL)
    spot = lax.rem(r // 4, QUAD)
    spot_next = lax.rem(nxt // 4, QUAD)
    far = lax.rem(r + 16, NL)
    z_up = lax.rem(z + 1, NZ)
    z_dn = lax.rem(z + NZ - 1, NZ)
    first_half = r < 16
    starts = jnp.logical_and(first_half, lax.rem(r, GROUP) == 0)
    starts_later = jnp.logical_and(first_half, lax.rem(r, GROUP) != 0)

    def phase(back):
        return lax.rem(r - back + 2 * GROUP, GROUP)

    def to(layer, src, dst, send, recv):
        return pltpu.make_async_remote_copy(
            src_ref=src, dst_ref=dst, send_sem=send, recv_sem=recv,
            device_id=(layer, z), device_id_type=MESH)

    loads = [
        pltpu.make_async_copy(
            w_ref.at[layer], wf.at[layer, pl.ds(pl.multiple_of(z * KR, KR), KR)], load_s.at[layer])
        for layer in range(LD)
    ]
    loads.append(pltpu.make_async_copy(b_ref, bias, load_s.at[LD]))
    guess_loads = [
        pltpu.make_async_copy(g_ref.at[0, :, pl.ds(c * LANES, LANES)], natural.at[c], load_s.at[LD + 1 + c])
        for c in range(D // LANES)
    ]
    for load in loads + guess_loads:
        load.start()

    def peer(d, i):
        j = lax.rem(d // 4, QUAD)
        other = j + 1 - 2 * lax.rem(j, 2) if i == 1 else lax.rem(j + 2, 4) if i == 2 else 3 - j
        return d + 4 * (other - j)

    barrier = pltpu.get_barrier_semaphore()
    greeted = [(r, z_up), (r, z_dn), (nxt, z), (prv, z), (far, z)]
    for i in range(1, QUAD):
        greeted += [
            (peer(r, i), z),
            (lax.rem(peer(r, i) + 1, NL), z), (peer(prv, i), z),
            (peer(nxt, i), z), (lax.rem(peer(r, i) + NL - 1, NL), z),
        ]
    for dev in greeted:
        pl.semaphore_signal(barrier, inc=1, device_id=dev, device_id_type=MESH)
    for load in loads:
        load.wait()
    pl.semaphore_wait(barrier, len(greeted))

    def shard(layer, origin):
        o = lax.rem(origin + 2 * NZ, NZ)
        return wf.at[layer, pl.ds(pl.multiple_of(o * KR, KR), KR)]

    def ring(way, step, layer, arrived=False):
        back = step if arrived else step - 1
        block = shard(layer, z - back if way == 0 else z + back)
        return pltpu.make_async_remote_copy(
            src_ref=block, dst_ref=block, send_sem=ring_s.at[way, step - 1, layer],
            recv_sem=ring_r.at[way, step - 1, layer],
            device_id=(r, z_up if way == 0 else z_dn), device_id_type=MESH)

    def owner(s):
        return r + 4 * (s - spot)

    def each_peer(action):
        for s in range(QUAD):
            @pl.when(s != spot)
            def _():
                action(s)

    def head_copy(s, slot, origin):
        o = lax.rem(origin + 2 * NZ, NZ)
        rows = pl.ds(pl.multiple_of(o * KR, KR), KR)
        return to(owner(s), wf.at[0, rows], heads.at[slot, rows], head_s.at[s, o], head_r.at[slot, o])

    mate = spot + 1 - 2 * lax.rem(spot, 2)
    across = lax.rem(spot + 2, QUAD)
    diagonal = 3 - spot

    def send_head(origin):
        head_copy(mate, spot, origin).start()
        head_copy(across, spot, origin).start()

    def head_hand_on(origin):
        o = lax.rem(origin + 2 * NZ, NZ)
        rows = pl.ds(pl.multiple_of(o * KR, KR), KR)
        return to(
            owner(across), heads.at[mate, rows], heads.at[mate, rows], head_s.at[diagonal, o], head_r.at[mate, o])

    def hand_on(origin):
        head_copy(mate, mate, origin).wait_recv()
        head_hand_on(origin).start()

    def bias_copy(s, slot):
        return to(owner(s), bias, hbias.at[slot], bias_s.at[s], bias_r.at[slot])

    def quarter(j):
        if not isinstance(j, int):
            return pl.ds(pl.multiple_of(j * QR, QR), QR)
        return pl.ds(j * QR, QR)

    def part_copy(s, slot):
        return to(owner(s), guess.at[phase(0), quarter(s)], part.at[slot], part_s.at[s], part_r.at[slot])

    def base_copy(m):
        src = guess.at[phase(0)] if m == 0 else base_in.at[m - 1]
        return to(nxt, src, base_in.at[m], base_s.at[m], base_r.at[m])

    def last_step(way, layer):
        return (layer < 2) == (way == 0)

    for layer in range(LD):
        for way in range(2):
            ring(way, 1, layer).start()
    send_head(z)
    each_peer(lambda s: bias_copy(s, spot).start())
    for c in range(D // LANES):
        guess_loads[c].wait()
        for p in range(GROUP):
            guess[p, :, pl.ds(c * LANES, LANES)] = natural[c, pl.ds(p, PR, stride=GROUP), :]

    @pl.when(r != NL - 1)
    def _():
        base_copy(0).start()

    each_peer(lambda s: part_copy(s, spot).start())
    part[spot] = guess[phase(0), quarter(spot), :]
    hbias[spot] = bias[...]

    @pl.when(r == 0)
    def _():
        for m in range(1, 4):
            base_in[m - 1] = guess[phase(m)]
            inc_in[m - 1] = jnp.zeros((PR, D), jnp.bfloat16)
        first_in[...] = guess[phase(1)]
        hop_in[0] = guess[phase(2)]
        hop_in[1] = guess[phase(3)]

    def ring_body(step, carry):
        for layer in range(LD):
            for way in range(2):
                ring(way, step, layer, True).wait_recv()
                ring(way, step + 1, layer).start()
                if layer == 0:
                    send_head(z - step if way == 0 else z + step)
        return carry

    def ring_and_hand_on(step, carry):
        ring_body(step, carry)
        hand_on(z - step + 2)
        hand_on(z + step - 2)
        return carry

    def far_copy(s):
        return to(nxt + 4 * s, base_in.at[2, quarter(s)], base_far, far_s.at[s], far_r.at[0])

    for m in range(3):
        lax.fori_loop(1 + 2 * m, 3 + 2 * m, ring_body if m == 0 else ring_and_hand_on, 0)
        if m == 0:
            hand_on(z)

        @pl.when(r != 0)
        def _():
            base_copy(m).wait_recv()

        if m < 2:
            @pl.when(r != NL - 1)
            def _():
                base_copy(m + 1).start()
        else:
            @pl.when(r < GROUP - 1)
            def _():
                for s in range(QUAD):
                    far_copy(s).start()

    for layer in range(LD):
        for way in range(2):
            ring(way, 7, layer, True).wait_recv()
            if last_step(way, layer):
                ring(way, 8, layer).start()
            if layer == 0:
                send_head(z - 7 if way == 0 else z + 7)

    hand_on(z - 5)
    hand_on(z + 5)

    def finish(layer):
        way = 0 if layer < 2 else 1
        ring(way, 8, layer, True).wait_recv()

    def act(u, weight, row):
        return jnp.tanh(jnp.dot(u.astype(jnp.bfloat16), weight, preferred_element_type=jnp.float32) + row)

    def bias_row(layer):
        return bias[pl.ds(layer, 1), :]

    finish(0)
    send_head(z - 8)
    own_head = pltpu.make_async_copy(wf.at[0], heads.at[spot], own_s.at[0])
    own_head.start()
    hand_on(z - 6)
    hand_on(z + 6)
    for back in range(GROUP):
        tau[phase(back)] = act(guess[phase(back)], wf[0], bias_row(0))

    def sweep(back, first_time=False):
        p = phase(back)
        start, first = guess[p], tau[p]
        inc = FINE * first
        for layer in range(1, LD):
            if first_time:
                finish(layer)
            inc = inc + FINE * act(start + inc, wf[layer], bias_row(layer))
        tau[p] = inc - BLOCK * first
        return inc

    def chunk(c):
        return pl.ds(c * HR, HR)

    def level_copy(m, c):
        return to(nxt, inc_out.at[m, chunk(c)], inc_in.at[m, chunk(c)], level_s.at[m, c], level_r.at[m, c])

    inc_out[0] = sweep(0, True).astype(jnp.bfloat16)

    @pl.when(r != NL - 1)
    def _():
        for c in range(2):
            level_copy(0, c).start()

    hand_on(z - 7)
    hand_on(z + 7)
    hand_on(z - 8)

    def arr_copy(s):
        return to(
            nxt + 4 * (s - spot_next), inc_out.at[3, quarter(s)], arr.at[spot_next], arr_s.at[s], arr_r.at[spot_next])

    for m in range(1, 4):
        sweep(m)
        p = phase(m)
        for c in range(2):
            @pl.when(r != 0)
            def _():
                level_copy(m - 1, c).wait_recv()

            before = inc_in[m - 1, chunk(c), :].astype(jnp.float32)
            u = base_in[m - 1, chunk(c), :] + before
            after = before + BLOCK * act(u, wf[0], bias_row(0)) + tau[p, chunk(c), :]
            inc_out[m, chunk(c), :] = after.astype(jnp.bfloat16)

            @pl.when(r != NL - 1)
            def _():
                if m < 3:
                    level_copy(m, c).start()
                else:
                    arr_copy(2 * c).start()
                    arr_copy(2 * c + 1).start()

    own_head.wait()

    def wait_from(s):
        def wait_head(o, carry):
            head_copy(s, s, o).wait_recv()
            return carry

        @pl.when(s != mate)
        def _():
            lax.fori_loop(0, NZ, wait_head, 0)

        bias_copy(s, s).wait_recv()
        part_copy(s, s).wait_recv()

    each_peer(wait_from)
    for s in range(QUAD):
        part_act[s] = act(part[s], heads[s], hbias[s, pl.ds(0, 1), :])

    def arrived(s):
        to(nxt, inc_out.at[3, quarter(s)], arr.at[s], arr_s.at[s], arr_r.at[s]).wait_recv()

    q_copy = to(far, coarse_out, coarse_in, q_s.at[0], q_r.at[0])

    @pl.when(starts)
    def _():
        coarse[0] = part[0]

    @pl.when(starts_later)
    def _():
        far_copy(0).wait_recv()
        arrived(0)
        coarse[0] = base_far[...] + arr[0].astype(jnp.float32)

    @pl.when(jnp.logical_not(first_half))
    def _():
        arrived(0)

    for s in range(1, QUAD):
        arrived(s)

    @pl.when(jnp.logical_not(first_half))
    def _():
        q_copy.wait_recv()
        coarse[0] = coarse_in[...] + arr[0].astype(jnp.float32)

    def first_copy(s, place):
        return to(
            lax.rem(owner(s) + 1, NL), first_out.at[s], first_in.at[quarter(place)], first_s.at[s], first_r.at[place])

    def corr_copy(s, place):
        return to(owner(s), coarse.at[s], corr_in.at[quarter(place)], corr_s.at[s], corr_r.at[place])

    u = coarse[0]
    for s in range(QUAD):
        change = act(u, heads[s], hbias[s, pl.ds(0, 1), :]) - part_act[s]
        following = u + WIDE * change
        if s == QUAD - 1:
            @pl.when(first_half)
            def _():
                coarse_out[...] = following
                q_copy.start()

        first_out[s] = u + BLOCK * change

        @pl.when(owner(s) != NL - 1)
        def _():
            first_copy(s, spot).start()

        @pl.when(s != spot)
        def _():
            corr_copy(s, spot).start()

        if s < QUAD - 1:
            u = following + arr[s + 1].astype(jnp.float32)
            coarse[s + 1] = u

    def put(p, offset, count, values):
        for c in range(D // LANES):
            fin[c, pl.ds(p + GROUP * offset, count, stride=GROUP), :] = values[:, c * LANES:(c + 1) * LANES]

    put(phase(0), spot * QR, QR, coarse[spot])

    def hop(m, c):
        return to(nxt, hop_out.at[m, chunk(c)], hop_in.at[m, chunk(c)], hop_s.at[m, c], hop_r.at[m, c])

    for m in range(1, 4):
        p = phase(m)
        for c in range(2):
            @pl.when(r != 0)
            def _():
                if m == 1:
                    first_copy(0, 2 * c).wait_recv()
                    first_copy(0, 2 * c + 1).wait_recv()
                else:
                    hop(m - 2, c).wait_recv()

            if m == 1:
                u = first_in[chunk(c), :] + inc_in[0, chunk(c), :].astype(jnp.float32)
            else:
                u = hop_in[m - 2, chunk(c), :]
            if m < 3:
                hop_out[m - 1, chunk(c), :] = u + BLOCK * act(u, wf[0], bias_row(0)) + tau[p, chunk(c), :]

                @pl.when(r != NL - 1)
                def _():
                    hop(m - 1, c).start()

            put(p, c * HR, HR, u)

    def take_corr(s):
        corr_copy(s, s).wait_recv()
        put(phase(0), s * QR, QR, corr_in[quarter(s), :])

    each_peer(take_corr)

    for tile in range(4):
        rows = pl.ds(tile * 128, 128)
        u = jnp.concatenate([fin[c, rows, :] for c in range(D // LANES)], axis=1)
        for layer in range(LD):
            u = u + FINE * act(u, wf[layer], bias_row(layer))
            o_ref[layer, rows, :] = u.astype(jnp.bfloat16)

    def drain(step, carry):
        for layer in range(LD):
            for way in range(2):
                ring(way, step, layer).wait_send()
        return carry

    lax.fori_loop(1, 8, drain, 0)
    for layer in range(LD):
        for way in range(2):
            if last_step(way, layer):
                ring(way, 8, layer).wait_send()

    def drain_peer(s):
        def drain_head(o, carry):
            head_copy(s, spot, o).wait_send()
            return carry

        lax.fori_loop(0, NZ, drain_head, 0)
        bias_copy(s, spot).wait_send()
        part_copy(s, spot).wait_send()
        corr_copy(s, spot).wait_send()

    each_peer(drain_peer)

    @pl.when(r != NL - 1)
    def _():
        for m in range(3):
            base_copy(m).wait_send()
            for c in range(2):
                level_copy(m, c).wait_send()
        for s in range(QUAD):
            arr_copy(s).wait_send()
        for m in range(2):
            for c in range(2):
                hop(m, c).wait_send()

    @pl.when(r < GROUP - 1)
    def _():
        for s in range(QUAD):
            far_copy(s).wait_send()

    @pl.when(first_half)
    def _():
        q_copy.wait_send()

    for s in range(QUAD):
        @pl.when(owner(s) != NL - 1)
        def _():
            first_copy(s, spot).wait_send()


def per_device(weights, biases, guesses):
    f32, bf16 = jnp.float32, jnp.bfloat16
    dma = pltpu.SemaphoreType.DMA
    hbm = pl.BlockSpec(memory_space=pltpu.HBM)
    scratch = dict(
        wf=pltpu.VMEM((LD, D, D), bf16),
        bias=pltpu.VMEM((LD, D), f32),
        natural=pltpu.VMEM((D // LANES, ROWS, LANES), f32),
        guess=pltpu.VMEM((GROUP, PR, D), f32),
        base_in=pltpu.VMEM((3, PR, D), f32),
        tau=pltpu.VMEM((GROUP, PR, D), f32),
        inc_in=pltpu.VMEM((3, PR, D), bf16),
        inc_out=pltpu.VMEM((4, PR, D), bf16),
        heads=pltpu.VMEM((QUAD, D, D), bf16),
        hbias=pltpu.VMEM((QUAD, LD, D), f32),
        part=pltpu.VMEM((QUAD, QR, D), f32),
        part_act=pltpu.VMEM((QUAD, QR, D), f32),
        arr=pltpu.VMEM((QUAD, QR, D), bf16),
        base_far=pltpu.VMEM((QR, D), f32),
        coarse_in=pltpu.VMEM((QR, D), f32),
        coarse_out=pltpu.VMEM((QR, D), f32),
        coarse=pltpu.VMEM((QUAD, QR, D), f32),
        corr_in=pltpu.VMEM((PR, D), f32),
        first_out=pltpu.VMEM((QUAD, QR, D), f32),
        first_in=pltpu.VMEM((PR, D), f32),
        hop_in=pltpu.VMEM((2, PR, D), f32),
        hop_out=pltpu.VMEM((2, PR, D), f32),
        fin=pltpu.VMEM((D // LANES, ROWS, LANES), f32),
        load_s=dma((LD + 1 + D // LANES,)),
        ring_s=dma((2, 8, LD)), ring_r=dma((2, 8, LD)),
        head_s=dma((QUAD, NZ)), head_r=dma((QUAD, NZ)),
        bias_s=dma((QUAD,)), bias_r=dma((QUAD,)),
        part_s=dma((QUAD,)), part_r=dma((QUAD,)),
        base_s=dma((3,)), base_r=dma((3,)),
        far_s=dma((QUAD,)), far_r=dma((1,)),
        level_s=dma((3, 2)), level_r=dma((3, 2)),
        arr_s=dma((QUAD,)), arr_r=dma((QUAD,)),
        q_s=dma((1,)), q_r=dma((1,)),
        corr_s=dma((QUAD,)), corr_r=dma((QUAD,)),
        first_s=dma((QUAD,)), first_r=dma((QUAD,)),
        hop_s=dma((2, 2)), hop_r=dma((2, 2)),
        own_s=dma((1,)),
    )
    return pl.pallas_call(
        kernel,
        out_shape=jax.ShapeDtypeStruct((LD, ROWS, D), bf16),
        in_specs=[hbm, hbm, hbm],
        out_specs=pl.BlockSpec(memory_space=pltpu.VMEM),
        scratch_shapes=scratch,
        compiler_params=pltpu.CompilerParams(
            collective_id=1, has_side_effects=True, vmem_limit_bytes=40 * 2**20),
        cost_estimate=pl.CostEstimate(flops=3 * 10**9, bytes_accessed=3 * 2**20, transcendentals=3 * 10**6),
    )(weights, biases, guesses)


def solution(mesh):
    in_specs = (P("layer", "dp", None), P("layer", None), P("layer", "dp", None))
    out_specs = P("layer", "dp", None)
    return jax.shard_map(
        per_device, mesh=mesh, in_specs=in_specs, out_specs=out_specs, check_vma=False
    )
```

time: 309 us -> 90.6 us (0.29)
  waiting for transfers between devices: 223 us -> 0 us
  Pallas kernels: 0 us -> 86.2 us
  starting transfers between devices: 47.7 us -> 0 us
  local copies, waits for them, and re-layouts: 19.2 us -> 4.15 us
  matrix products: 9.75 us -> 0 us
  other arithmetic: 7.5 us -> 0 us
    ppermute x16 -> x0, waiting for transfers between devices: 128 us -> none  [from_behind(): lax.ppermute(value, axis, [(source, source + steps) for source in range(i...]
    all_to_all x1 -> x0, waiting for transfers between devices: 95.6 us -> none  [copy_for_each(): lax.all_to_all(jnp.broadcast_to(x[None], (count, *x.shape)), axis, 0, 0,...]
    pallas_call x0 -> x1, Pallas kernels: none -> 86.2 us  [per_device(): pl.pallas_call(kernel, out_shape=jax.ShapeDtypeStruct((LD, ROWS, D), bf16...]
    ppermute x16 -> x0, starting transfers between devices: 32.4 us -> none  [from_behind(): lax.ppermute(value, axis, [(source, source + steps) for source in range(i...]
    all_to_all x1 -> x0, starting transfers between devices: 15.3 us -> none  [copy_for_each(): lax.all_to_all(jnp.broadcast_to(x[None], (count, *x.shape)), axis, 0, 0,...]
    dot_general x22 -> x0, matrix products: 9.75 us -> none  [advance(): jnp.dot(states_in.astype(jnp.bfloat16), weight_mat, preferred_element_typ...]
    dynamic_slice x1 -> x0, local copies, waits for them, and re-layouts: 4.37 us -> none  [take_phase(): return lax.dynamic_index_in_dim(grouped, phase, 1, keepdims=False)]
    select_n x13 -> x0, other arithmetic: 3.31 us -> none  [the longest x3 1.38 us: per_device(): level = jnp.where(layer_rank >= 1, put_phase(level, landing, moved), level)]
  transfers between devices with their start and end apart: 17 -> 0, of which waited for: 15 -> 0; matrix products, arithmetic and copies ran while one was open for 4% -> 0% of each run, Pallas kernels for 0% -> 0%
where the time goes in v2:
time: 90.6 us; the launch traced here: 90.4 us
  Pallas kernels  86.2 us (95%)
  local copies, waits for them, and re-layouts  4.15 us (5%)
    pallas_call x1, Pallas kernels, per_device(): pl.pallas_call(kernel, out_shape=jax.ShapeDtypeStruct((LD, ROWS, D), bf16...  86.2 us
    unnamed x7, local copies, waits for them, and re-layouts  4.15 us

profile of v2, /device:TPU:6, one launch (start us, length us, event | category | flops | bytes accessed | tf_op | source)
XLA Modules:
  0.0 90.4 jit_solution(6330926812786605478)
XLA Ops:
  0.0 0.0 copy-start
  0.0 1.2 %copy-done = f32[1,512,512]{2,1,0:T(8,128)S(1)} copy-done((f32[1,512,512]{2,1,0:T(8,128)S(1)}, f32[1,512,512]{2,1,0:T(8,128)}, u32[]{:S(2)}) %copy-start) | copy-done | bytes 1048600
  1.2 0.0 copy-start.1
  1.2 0.9 copy-done.1
  2.1 0.0 copy-start.2
  2.1 0.7 copy-done.2
  2.8 86.2 %shard_map.37 = bf16[4,512,512]{2,1,0:T(8,128)(2,1)S(1)} custom-call(bf16[4,32,512]{2,1,0:T(8,128)(2,1)S(1)} %copy-done.1, f32[4,512]{1,0:T(4,128)S(1)} %copy-done.2, f32[1,512,512]{2,1,0:T(8,128)S(1)} %copy-done), custom_call_target="tpu_custom_call" | custom-call | flops 3000000000 | bytes 3145728 | tf_op jit(solution)/shard_map/pallas_call | solution.py:511
  89.1 1.3 %copy.5 = bf16[4,512,512]{2,1,0:T(8,128)(2,1)} copy(bf16[4,512,512]{2,1,0:T(8,128)(2,1)S(1)} %shard_map.37) | data formatting | bytes 4194304
Async XLA Ops:
  0.0 1.2 %copy-start = (f32[1,512,512]{2,1,0:T(8,128)S(1)}, f32[1,512,512]{2,1,0:T(8,128)}, u32[]{:S(2)}) copy-start(f32[1,512,512]{2,1,0:T(8,128)} %g_ref.1) | copy-start | bytes 3145732
  1.2 0.9 %copy-start.1 = (bf16[4,32,512]{2,1,0:T(8,128)(2,1)S(1)}, bf16[4,32,512]{2,1,0:T(8,128)(2,1)}, u32[]{:S(2)}) copy-start(bf16[4,32,512]{2,1,0:T(8,128)(2,1)} %w_ref.1) | copy-start | bytes 393220
  2.1 0.7 copy-start.2

commit v3 on v2

--- a/solution.py
+++ b/solution.py
@@ -26,9 +26,9 @@
 def kernel(
     w_ref, b_ref, g_ref, o_ref,
     wf, bias, natural, guess, base_in, tau, inc_in, inc_out, heads, hbias, part, part_act, arr, base_far,
-    coarse_in, coarse_out, coarse, corr_in, first_out, first_in, hop_in, hop_out, fin,
+    coarse_in, coarse_out, coarse, corr_in, first_out, first_in, hop_in, hop_out, fin, first_now,
     load_s, ring_s, ring_r, head_s, head_r, bias_s, bias_r, part_s, part_r, base_s, base_r, far_s, far_r,
-    level_s, level_r, arr_s, arr_r, q_s, q_r, corr_s, corr_r, first_s, first_r, hop_s, hop_r, own_s,
+    level_s, level_r, arr_s, arr_r, q_s, q_r, corr_s, corr_r, first_s, first_r, hop_s, hop_r, own_s, done, out_s,
 ):
     r = lax.axis_index("layer")
     z = lax.axis_index("dp")
@@ -37,8 +37,6 @@
     spot = lax.rem(r // 4, QUAD)
     spot_next = lax.rem(nxt // 4, QUAD)
     far = lax.rem(r + 16, NL)
-    z_up = lax.rem(z + 1, NZ)
-    z_dn = lax.rem(z + NZ - 1, NZ)
     first_half = r < 16
     starts = jnp.logical_and(first_half, lax.rem(r, GROUP) == 0)
     starts_later = jnp.logical_and(first_half, lax.rem(r, GROUP) != 0)
@@ -70,7 +68,8 @@
         return d + 4 * (other - j)
 
     barrier = pltpu.get_barrier_semaphore()
-    greeted = [(r, z_up), (r, z_dn), (nxt, z), (prv, z), (far, z)]
+    greeted = [(r, lax.rem(z + d, NZ)) for d in (1, NZ - 1)]
+    greeted += [(nxt, z), (prv, z), (far, z)]
     for i in range(1, QUAD):
         greeted += [
             (peer(r, i), z),
@@ -93,7 +92,7 @@
         return pltpu.make_async_remote_copy(
             src_ref=block, dst_ref=block, send_sem=ring_s.at[way, step - 1, layer],
             recv_sem=ring_r.at[way, step - 1, layer],
-            device_id=(r, z_up if way == 0 else z_dn), device_id_type=MESH)
+            device_id=(r, lax.rem(z + (1 if way == 0 else NZ - 1), NZ)), device_id_type=MESH)
 
     def owner(s):
         return r + 4 * (s - spot)
@@ -183,8 +182,12 @@
 
     def ring_and_hand_on(step, carry):
         ring_body(step, carry)
-        hand_on(z - step + 2)
-        hand_on(z + step - 2)
+        hand_on(z - step + 3)
+
+        @pl.when(step > 3)
+        def _():
+            hand_on(z + step - 3)
+
         return carry
 
     def far_copy(s):
@@ -192,8 +195,6 @@
 
     for m in range(3):
         lax.fori_loop(1 + 2 * m, 3 + 2 * m, ring_body if m == 0 else ring_and_hand_on, 0)
-        if m == 0:
-            hand_on(z)
 
         @pl.when(r != 0)
         def _():
@@ -217,8 +218,8 @@
             if layer == 0:
                 send_head(z - 7 if way == 0 else z + 7)
 
-    hand_on(z - 5)
-    hand_on(z + 5)
+    hand_on(z - 4)
+    hand_on(z + 4)
 
     def finish(layer):
         way = 0 if layer < 2 else 1
@@ -234,14 +235,11 @@
     send_head(z - 8)
     own_head = pltpu.make_async_copy(wf.at[0], heads.at[spot], own_s.at[0])
     own_head.start()
-    hand_on(z - 6)
-    hand_on(z + 6)
-    for back in range(GROUP):
-        tau[phase(back)] = act(guess[phase(back)], wf[0], bias_row(0))
 
     def sweep(back, first_time=False):
         p = phase(back)
-        start, first = guess[p], tau[p]
+        start = guess[p]
+        first = act(start, wf[0], bias_row(0))
         inc = FINE * first
         for layer in range(1, LD):
             if first_time:
@@ -263,9 +261,6 @@
         for c in range(2):
             level_copy(0, c).start()
 
-    hand_on(z - 7)
-    hand_on(z + 7)
-    hand_on(z - 8)
 
     def arr_copy(s):
         return to(
@@ -291,6 +286,15 @@
                 else:
                     arr_copy(2 * c).start()
                     arr_copy(2 * c + 1).start()
+
+        if m == 1:
+            for back in (5, 6):
+                hand_on(z - back)
+                hand_on(z + back)
+        elif m == 2:
+            hand_on(z - 7)
+            hand_on(z + 7)
+            hand_on(z - 8)
 
     own_head.wait()
 
@@ -356,63 +360,75 @@
 
         first_out[s] = u + BLOCK * change
 
-        @pl.when(owner(s) != NL - 1)
+        @pl.when(jnp.logical_and(jnp.logical_not(first_half), owner(s) != NL - 1))
         def _():
             first_copy(s, spot).start()
-
-        @pl.when(s != spot)
-        def _():
-            corr_copy(s, spot).start()
 
         if s < QUAD - 1:
             u = following + arr[s + 1].astype(jnp.float32)
             coarse[s + 1] = u
 
-    def put(p, offset, count, values):
+    for s in range(QUAD):
+        @pl.when(first_half)
+        def _():
+            first_copy(s, spot).start()
+
+    each_peer(lambda s: corr_copy(s, spot).start())
+
+    def put(layer, p, values):
         for c in range(D // LANES):
-            fin[c, pl.ds(p + GROUP * offset, count, stride=GROUP), :] = values[:, c * LANES:(c + 1) * LANES]
-
-    put(phase(0), spot * QR, QR, coarse[spot])
+            fin[layer, c, pl.ds(p, PR, stride=GROUP), :] = values[:, c * LANES:(c + 1) * LANES]
+
+    def settle(back, u):
+        for layer in range(LD):
+            u = u + FINE * act(u, wf[layer], bias_row(layer))
+            put(layer, phase(back), u)
+
+    corr_in[quarter(spot), :] = coarse[spot]
 
     def hop(m, c):
-        return to(nxt, hop_out.at[m, chunk(c)], hop_in.at[m, chunk(c)], hop_s.at[m, c], hop_r.at[m, c])
+        return to(nxt, hop_out.at[m, quarter(c)], hop_in.at[m, quarter(c)], hop_s.at[m, c], hop_r.at[m, c])
 
     for m in range(1, 4):
         p = phase(m)
-        for c in range(2):
+        for c in range(QUAD):
             @pl.when(r != 0)
             def _():
                 if m == 1:
-                    first_copy(0, 2 * c).wait_recv()
-                    first_copy(0, 2 * c + 1).wait_recv()
+                    first_copy(0, c).wait_recv()
                 else:
                     hop(m - 2, c).wait_recv()
 
             if m == 1:
-                u = first_in[chunk(c), :] + inc_in[0, chunk(c), :].astype(jnp.float32)
-            else:
-                u = hop_in[m - 2, chunk(c), :]
+                u = first_in[quarter(c), :] + inc_in[0, quarter(c), :].astype(jnp.float32)
+                first_now[quarter(c), :] = u
+            elif m == 2:
+                u = hop_in[0, quarter(c), :]
             if m < 3:
-                hop_out[m - 1, chunk(c), :] = u + BLOCK * act(u, wf[0], bias_row(0)) + tau[p, chunk(c), :]
+                hop_out[m - 1, quarter(c), :] = u + BLOCK * act(u, wf[0], bias_row(0)) + tau[p, quarter(c), :]
 
                 @pl.when(r != NL - 1)
                 def _():
                     hop(m - 1, c).start()
 
-            put(p, c * HR, HR, u)
-
-    def take_corr(s):
-        corr_copy(s, s).wait_recv()
-        put(phase(0), s * QR, QR, corr_in[quarter(s), :])
-
-    each_peer(take_corr)
-
-    for tile in range(4):
+        if m == 1:
+            settle(1, first_now[...])
+        else:
+            settle(m, hop_in[m - 2])
+        if m == 2:
+            each_peer(lambda s: corr_copy(s, s).wait_recv())
+            settle(0, corr_in[...])
+
+    def out_copy(tile, layer):
         rows = pl.ds(tile * 128, 128)
-        u = jnp.concatenate([fin[c, rows, :] for c in range(D // LANES)], axis=1)
-        for layer in range(LD):
-            u = u + FINE * act(u, wf[layer], bias_row(layer))
-            o_ref[layer, rows, :] = u.astype(jnp.bfloat16)
+        return pltpu.make_async_copy(done.at[layer, rows], o_ref.at[layer, rows], out_s.at[tile, layer])
+
+    for layer in range(LD):
+        for tile in range(4):
+            rows = pl.ds(tile * 128, 128)
+            for c in range(D // LANES):
+                done[layer, rows, pl.ds(c * LANES, LANES)] = fin[layer, c, rows, :].astype(jnp.bfloat16)
+            out_copy(tile, layer).start()
 
     def drain(step, carry):
         for layer in range(LD):
@@ -447,7 +463,7 @@
         for s in range(QUAD):
             arr_copy(s).wait_send()
         for m in range(2):
-            for c in range(2):
+            for c in range(QUAD):
                 hop(m, c).wait_send()
 
     @pl.when(r < GROUP - 1)
@@ -463,6 +479,10 @@
         @pl.when(owner(s) != NL - 1)
         def _():
             first_copy(s, spot).wait_send()
+
+    for tile in range(4):
+        for layer in range(LD):
+            out_copy(tile, layer).wait()
 
 
 def per_device(weights, biases, guesses):
@@ -492,7 +512,8 @@
         first_in=pltpu.VMEM((PR, D), f32),
         hop_in=pltpu.VMEM((2, PR, D), f32),
         hop_out=pltpu.VMEM((2, PR, D), f32),
-        fin=pltpu.VMEM((D // LANES, ROWS, LANES), f32),
+        fin=pltpu.VMEM((LD, D // LANES, ROWS, LANES), f32),
+        first_now=pltpu.VMEM((PR, D), f32),
         load_s=dma((LD + 1 + D // LANES,)),
         ring_s=dma((2, 8, LD)), ring_r=dma((2, 8, LD)),
         head_s=dma((QUAD, NZ)), head_r=dma((QUAD, NZ)),
@@ -505,17 +526,19 @@
         q_s=dma((1,)), q_r=dma((1,)),
         corr_s=dma((QUAD,)), corr_r=dma((QUAD,)),
         first_s=dma((QUAD,)), first_r=dma((QUAD,)),
-        hop_s=dma((2, 2)), hop_r=dma((2, 2)),
+        hop_s=dma((2, QUAD)), hop_r=dma((2, QUAD)),
         own_s=dma((1,)),
+        done=pltpu.VMEM((LD, ROWS, D), bf16),
+        out_s=dma((4, LD)),
     )
     return pl.pallas_call(
         kernel,
         out_shape=jax.ShapeDtypeStruct((LD, ROWS, D), bf16),
         in_specs=[hbm, hbm, hbm],
-        out_specs=pl.BlockSpec(memory_space=pltpu.VMEM),
+        out_specs=hbm,
         scratch_shapes=scratch,
         compiler_params=pltpu.CompilerParams(
-            collective_id=1, has_side_effects=True, vmem_limit_bytes=40 * 2**20),
+            collective_id=1, has_side_effects=True, vmem_limit_bytes=56 * 2**20),
         cost_estimate=pl.CostEstimate(flops=3 * 10**9, bytes_accessed=3 * 2**20, transcendentals=3 * 10**6),
     )(weights, biases, guesses)
 

time: 90.6 us -> 81.5 us (0.90)
  Pallas kernels: 86.2 us -> 78.3 us
  local copies, waits for them, and re-layouts: 4.15 us -> 3.05 us
    pallas_call x1, Pallas kernels: 86.2 us -> 78.3 us  [per_device(): pl.pallas_call(kernel, out_shape=jax.ShapeDtypeStruct((LD, ROWS, D), bf16...]
    unnamed x7 -> x1, local copies, waits for them, and re-layouts: 4.15 us -> 3.05 us
where the time goes in v3:
time: 81.5 us; the launch traced here: 81.4 us
  Pallas kernels  78.3 us (96%)
  local copies, waits for them, and re-layouts  3.05 us (4%)
    pallas_call x1, Pallas kernels, per_device(): pl.pallas_call(kernel, out_shape=jax.ShapeDtypeStruct((LD, ROWS, D), bf16...  78.3 us
    unnamed x1, local copies, waits for them, and re-layouts  3.05 us

profile of v3, /device:TPU:6, one launch (start us, length us, event | category | flops | bytes accessed | tf_op | source)
XLA Modules:
  0.0 81.4 jit_solution(1287664662912706184)
XLA Ops:
  0.0 78.3 %shard_map.37 = bf16[4,512,512]{2,1,0:T(8,128)(2,1)} custom-call(bf16[4,32,512]{2,1,0:T(8,128)(2,1)} %w_ref.1, f32[4,512]{1,0:T(4,128)} %b_ref.1, f32[1,512,512]{2,1,0:T(8,128)} %g_ref.1), custom_call_target="tpu_custom_call" | custom-call | flops 3000000000 | bytes 3145728 | tf_op jit(solution)/shard_map/pallas_call | solution.py:534
  78.3 3.0 %copy.5 = bf16[4,512,512]{2,1,0:T(8,128)(2,1)} copy(bf16[4,512,512]{2,1,0:T(8,128)(2,1)} %shard_map.37) | data formatting | bytes 4194304

commit v4 on v3

--- a/solution.py
+++ b/solution.py
@@ -36,8 +36,11 @@
     prv = lax.rem(r + NL - 1, NL)
     spot = lax.rem(r // 4, QUAD)
     spot_next = lax.rem(nxt // 4, QUAD)
-    far = lax.rem(r + 16, NL)
     first_half = r < 16
+    turn = 2 * (r // 16)
+    turn_next = 2 * (nxt // 16)
+    outer = lax.rem(spot // 2 + r // 16, 2)
+    far = lax.rem(r + 24 - 16 * outer + (r // 16) * (32 * outer - 16), NL)
     starts = jnp.logical_and(first_half, lax.rem(r, GROUP) == 0)
     starts_later = jnp.logical_and(first_half, lax.rem(r, GROUP) != 0)
 
@@ -135,7 +138,7 @@
         return pl.ds(j * QR, QR)
 
     def part_copy(s, slot):
-        return to(owner(s), guess.at[phase(0), quarter(s)], part.at[slot], part_s.at[s], part_r.at[slot])
+        return to(owner(s), guess.at[phase(0), quarter(lax.rem(s + turn, QUAD))], part.at[slot], part_s.at[s], part_r.at[slot])
 
     def base_copy(m):
         src = guess.at[phase(0)] if m == 0 else base_in.at[m - 1]
@@ -159,7 +162,8 @@
         base_copy(0).start()
 
     each_peer(lambda s: part_copy(s, spot).start())
-    part[spot] = guess[phase(0), quarter(spot), :]
+    rows_here = lax.rem(spot + turn, QUAD)
+    part[spot] = guess[phase(0), quarter(rows_here), :]
     hbias[spot] = bias[...]
 
     @pl.when(r == 0)
@@ -167,9 +171,9 @@
         for m in range(1, 4):
             base_in[m - 1] = guess[phase(m)]
             inc_in[m - 1] = jnp.zeros((PR, D), jnp.bfloat16)
-        first_in[...] = guess[phase(1)]
-        hop_in[0] = guess[phase(2)]
-        hop_in[1] = guess[phase(3)]
+        first_in[...] = guess[phase(1)].astype(jnp.bfloat16)
+        hop_in[0] = guess[phase(2)].astype(jnp.bfloat16)
+        hop_in[1] = guess[phase(3)].astype(jnp.bfloat16)
 
     def ring_body(step, carry):
         for layer in range(LD):
@@ -264,7 +268,7 @@
 
     def arr_copy(s):
         return to(
-            nxt + 4 * (s - spot_next), inc_out.at[3, quarter(s)], arr.at[spot_next], arr_s.at[s], arr_r.at[spot_next])
+            nxt + 4 * (lax.rem(s + turn_next, QUAD) - spot_next), inc_out.at[3, quarter(s)], arr.at[spot_next], arr_s.at[s], arr_r.at[spot_next])
 
     for m in range(1, 4):
         sweep(m)
@@ -358,11 +362,11 @@
                 coarse_out[...] = following
                 q_copy.start()
 
-        first_out[s] = u + BLOCK * change
+        first_out[s] = (u + BLOCK * change).astype(jnp.bfloat16)
 
         @pl.when(jnp.logical_and(jnp.logical_not(first_half), owner(s) != NL - 1))
         def _():
-            first_copy(s, spot).start()
+            first_copy(s, rows_here).start()
 
         if s < QUAD - 1:
             u = following + arr[s + 1].astype(jnp.float32)
@@ -371,9 +375,9 @@
     for s in range(QUAD):
         @pl.when(first_half)
         def _():
-            first_copy(s, spot).start()
-
-    each_peer(lambda s: corr_copy(s, spot).start())
+            first_copy(s, rows_here).start()
+
+    each_peer(lambda s: corr_copy(s, rows_here).start())
 
     def put(layer, p, values):
         for c in range(D // LANES):
@@ -384,7 +388,7 @@
             u = u + FINE * act(u, wf[layer], bias_row(layer))
             put(layer, phase(back), u)
 
-    corr_in[quarter(spot), :] = coarse[spot]
+    corr_in[quarter(rows_here), :] = coarse[spot]
 
     def hop(m, c):
         return to(nxt, hop_out.at[m, quarter(c)], hop_in.at[m, quarter(c)], hop_s.at[m, c], hop_r.at[m, c])
@@ -400,12 +404,13 @@
                     hop(m - 2, c).wait_recv()
 
             if m == 1:
-                u = first_in[quarter(c), :] + inc_in[0, quarter(c), :].astype(jnp.float32)
+                u = first_in[quarter(c), :].astype(jnp.float32) + inc_in[0, quarter(c), :].astype(jnp.float32)
                 first_now[quarter(c), :] = u
             elif m == 2:
-                u = hop_in[0, quarter(c), :]
+                u = hop_in[0, quarter(c), :].astype(jnp.float32)
             if m < 3:
-                hop_out[m - 1, quarter(c), :] = u + BLOCK * act(u, wf[0], bias_row(0)) + tau[p, quarter(c), :]
+                after = u + BLOCK * act(u, wf[0], bias_row(0)) + tau[p, quarter(c), :]
+                hop_out[m - 1, quarter(c), :] = after.astype(jnp.bfloat16)
 
                 @pl.when(r != NL - 1)
                 def _():
@@ -414,9 +419,9 @@
         if m == 1:
             settle(1, first_now[...])
         else:
-            settle(m, hop_in[m - 2])
+            settle(m, hop_in[m - 2].astype(jnp.float32))
         if m == 2:
-            each_peer(lambda s: corr_copy(s, s).wait_recv())
+            each_peer(lambda s: corr_copy(s, lax.rem(s + turn, QUAD)).wait_recv())
             settle(0, corr_in[...])
 
     def out_copy(tile, layer):
@@ -450,7 +455,7 @@
         lax.fori_loop(0, NZ, drain_head, 0)
         bias_copy(s, spot).wait_send()
         part_copy(s, spot).wait_send()
-        corr_copy(s, spot).wait_send()
+        corr_copy(s, rows_here).wait_send()
 
     each_peer(drain_peer)
 
@@ -478,7 +483,7 @@
     for s in range(QUAD):
         @pl.when(owner(s) != NL - 1)
         def _():
-            first_copy(s, spot).wait_send()
+            first_copy(s, rows_here).wait_send()
 
     for tile in range(4):
         for layer in range(LD):
@@ -508,10 +513,10 @@
         coarse_out=pltpu.VMEM((QR, D), f32),
         coarse=pltpu.VMEM((QUAD, QR, D), f32),
         corr_in=pltpu.VMEM((PR, D), f32),
-        first_out=pltpu.VMEM((QUAD, QR, D), f32),
-        first_in=pltpu.VMEM((PR, D), f32),
-        hop_in=pltpu.VMEM((2, PR, D), f32),
-        hop_out=pltpu.VMEM((2, PR, D), f32),
+        first_out=pltpu.VMEM((QUAD, QR, D), bf16),
+        first_in=pltpu.VMEM((PR, D), bf16),
+        hop_in=pltpu.VMEM((2, PR, D), bf16),
+        hop_out=pltpu.VMEM((2, PR, D), bf16),
         fin=pltpu.VMEM((LD, D // LANES, ROWS, LANES), f32),
         first_now=pltpu.VMEM((PR, D), f32),
         load_s=dma((LD + 1 + D // LANES,)),

time: 81.5 us -> 77.7 us (0.953)
  Pallas kernels: 78.3 us -> 74.5 us
    pallas_call x1, Pallas kernels: 78.3 us -> 74.5 us  [per_device(): pl.pallas_call(kernel, out_shape=jax.ShapeDtypeStruct((LD, ROWS, D), bf16...]
where the time goes in v4:
time: 77.7 us; the launch traced here: 77.5 us
  Pallas kernels  74.5 us (96%)
  local copies, waits for them, and re-layouts  3.05 us (4%)
    pallas_call x1, Pallas kernels, per_device(): pl.pallas_call(kernel, out_shape=jax.ShapeDtypeStruct((LD, ROWS, D), bf16...  74.5 us
    unnamed x1, local copies, waits for them, and re-layouts  3.05 us

profile of v4, /device:TPU:6, one launch (start us, length us, event | category | flops | bytes accessed | tf_op | source)
XLA Modules:
  0.0 77.5 jit_solution(17942459359699185709)
XLA Ops:
  0.0 74.5 %shard_map.37 = bf16[4,512,512]{2,1,0:T(8,128)(2,1)} custom-call(bf16[4,32,512]{2,1,0:T(8,128)(2,1)} %w_ref.1, f32[4,512]{1,0:T(4,128)} %b_ref.1, f32[1,512,512]{2,1,0:T(8,128)} %g_ref.1), custom_call_target="tpu_custom_call" | custom-call | flops 3000000000 | bytes 3145728 | tf_op jit(solution)/shard_map/pallas_call | solution.py:539
  74.5 3.0 %copy.5 = bf16[4,512,512]{2,1,0:T(8,128)(2,1)} copy(bf16[4,512,512]{2,1,0:T(8,128)(2,1)} %shard_map.37) | data formatting | bytes 4194304

commit v5 on v4

--- a/solution.py
+++ b/solution.py
@@ -253,7 +253,7 @@
         return inc
 
     def chunk(c):
-        return pl.ds(c * HR, HR)
+        return pl.ds(c * QR, QR)
 
     def level_copy(m, c):
         return to(nxt, inc_out.at[m, chunk(c)], inc_in.at[m, chunk(c)], level_s.at[m, c], level_r.at[m, c])
@@ -262,7 +262,7 @@
 
     @pl.when(r != NL - 1)
     def _():
-        for c in range(2):
+        for c in range(QUAD):
             level_copy(0, c).start()
 
 
@@ -273,7 +273,7 @@
     for m in range(1, 4):
         sweep(m)
         p = phase(m)
-        for c in range(2):
+        for c in range(QUAD):
             @pl.when(r != 0)
             def _():
                 level_copy(m - 1, c).wait_recv()
@@ -288,8 +288,7 @@
                 if m < 3:
                     level_copy(m, c).start()
                 else:
-                    arr_copy(2 * c).start()
-                    arr_copy(2 * c + 1).start()
+                    arr_copy(c).start()
 
         if m == 1:
             for back in (5, 6):
@@ -463,7 +462,7 @@
     def _():
         for m in range(3):
             base_copy(m).wait_send()
-            for c in range(2):
+            for c in range(QUAD):
                 level_copy(m, c).wait_send()
         for s in range(QUAD):
             arr_copy(s).wait_send()
@@ -526,7 +525,7 @@
         part_s=dma((QUAD,)), part_r=dma((QUAD,)),
         base_s=dma((3,)), base_r=dma((3,)),
         far_s=dma((QUAD,)), far_r=dma((1,)),
-        level_s=dma((3, 2)), level_r=dma((3, 2)),
+        level_s=dma((3, QUAD)), level_r=dma((3, QUAD)),
         arr_s=dma((QUAD,)), arr_r=dma((QUAD,)),
         q_s=dma((1,)), q_r=dma((1,)),
         corr_s=dma((QUAD,)), corr_r=dma((QUAD,)),

time: 77.7 us -> 77 us (level)
  no operation moved by 1% of the time
where the time goes in v5:
time: 77 us; the launch traced here: 76.8 us
  Pallas kernels  73.8 us (96%)
  local copies, waits for them, and re-layouts  3.05 us (4%)
    pallas_call x1, Pallas kernels, per_device(): pl.pallas_call(kernel, out_shape=jax.ShapeDtypeStruct((LD, ROWS, D), bf16...  73.8 us
    unnamed x1, local copies, waits for them, and re-layouts  3.05 us

profile of v5, /device:TPU:6, one launch (start us, length us, event | category | flops | bytes accessed | tf_op | source)
XLA Modules:
  0.0 76.8 jit_solution(10681926281722865782)
XLA Ops:
  0.0 73.8 %shard_map.37 = bf16[4,512,512]{2,1,0:T(8,128)(2,1)} custom-call(bf16[4,32,512]{2,1,0:T(8,128)(2,1)} %w_ref.1, f32[4,512]{1,0:T(4,128)} %b_ref.1, f32[1,512,512]{2,1,0:T(8,128)} %g_ref.1), custom_call_target="tpu_custom_call" | custom-call | flops 3000000000 | bytes 3145728 | tf_op jit(solution)/shard_map/pallas_call | solution.py:538
  73.8 3.0 %copy.5 = bf16[4,512,512]{2,1,0:T(8,128)(2,1)} copy(bf16[4,512,512]{2,1,0:T(8,128)(2,1)} %shard_map.37) | data formatting | bytes 4194304
